TPU v7x, 512 devices: a whole 4x8x8 slice. The times are simulated.
512 devices in a mesh: wide: 16 (over y, core), narrow: 32 (over z, x).
Axes of the slice: x: 4, y: 8, z: 8, core: 2. Of those that a mesh axis runs over, the one named last changes fastest.
Arguments:
- embeddings: bfloat16 [12288, 1024], P(('wide', 'narrow')), may hold values from -6 to 6
- cluster: int32 [512], replicated, may hold values from 0 to 44, never falling along the last dimension, each value on 1 to 34 neighbouring positions
Outputs:
- shifted: float32 [12288, 1024], P(('wide', 'narrow'))
Inputs may be any that keep to these rules, and one draw needn't show every extreme that they name: The blocks of one cluster are consecutive (ids never fall); each cluster holds 1 to 34 blocks, one exactly 34.
All inputs are finite; a program needn't handle non-finite values.
Results may differ from a plain program's by a relative error of at most 0.029.
Values may be sent and summed in bfloat16 or wider, within the bound.
A program may use at most 64 MiB of HBM per device.

v0:
```python
import math
import jax
import jax.numpy as jnp
from jax import lax
from jax.sharding import PartitionSpec as P

D = 1024
REACH = 2
SPREAD = 0.5


def from_behind(block, axis, distance):
    devices = range(lax.axis_size(axis))
    route = [(i - distance, i) for i in devices if i - distance in devices]
    return lax.ppermute(block, axis, route)


def normalize(rows):
    values = rows.astype(jnp.float32)
    factor = lax.rsqrt(jnp.mean(values * values, axis=1, keepdims=True) + 1e-06)
    return (values * factor).astype(jnp.bfloat16)


def tile_weights(group, keys, row_clusters, key_cluster, self_start):
    scores = lax.dot_general(
        group, keys, (((1,), (1,)), ((), ())), preferred_element_type=jnp.float32
    )
    weights = jnp.exp(scores * (1.0 / (SPREAD * math.sqrt(D))))
    keep = row_clusters[:, None] == key_cluster
    if self_start is not None:
        query_rows = lax.broadcasted_iota(jnp.int32, scores.shape, 0)
        key_rows = lax.broadcasted_iota(jnp.int32, scores.shape, 1) + self_start
        keep = keep & (query_rows != key_rows)
    return jnp.where(keep, weights, jnp.float32(0.0))


def on_device(embeddings, cluster):
    blk = embeddings.shape[0]
    n_narrow = lax.axis_size("narrow")
    n_wide = lax.axis_size("wide")
    wide_at = lax.axis_index("wide")
    narrow_at = lax.axis_index("narrow")
    normed = normalize(embeddings)
    group = lax.all_gather(normed, "narrow", axis=0, tiled=True)
    rows_all = group.shape[0]
    first_block = wide_at * n_narrow
    group_clusters = lax.dynamic_slice_in_dim(cluster, first_block, n_narrow)
    row_clusters = jnp.broadcast_to(group_clusters[:, None], (n_narrow, blk)).reshape(rows_all)
    own_block = first_block + narrow_at

    def block_cluster(offset):
        target = wide_at + offset
        inside = (target >= 0) & (target < n_wide)
        position = jnp.clip(own_block + offset * n_narrow, 0, cluster.shape[0] - 1)
        found = lax.dynamic_index_in_dim(cluster, position, 0, keepdims=False)
        return jnp.where(inside, found, -1)

    def forward(keys, key_cluster, self_start):
        weights = tile_weights(group, keys, row_clusters, key_cluster, self_start)
        added = jnp.dot(weights.astype(jnp.bfloat16), keys, preferred_element_type=jnp.float32)
        return (added, jnp.sum(weights, axis=1))

    numerator, total = forward(normed, block_cluster(0), narrow_at * blk)
    for offset in range(-REACH, REACH + 1):
        if offset != 0:
            keys = from_behind(normed, "wide", -offset)
            added, summed = forward(keys, block_cluster(offset), None)
            numerator = numerator + added
            total = total + summed
    own_numerator, own_total = (
        lax.psum_scatter(
            numerator.astype(jnp.bfloat16), "narrow", scatter_dimension=0, tiled=True
        ).astype(jnp.float32),
        lax.psum_scatter(
            total.astype(jnp.bfloat16), "narrow", scatter_dimension=0, tiled=True
        ).astype(jnp.float32),
    )
    return own_numerator / own_total[:, None]


def solution(mesh):
    in_specs = (P(("wide", "narrow"), None), P())
    out_specs = P(("wide", "narrow"), None)
    return jax.shard_map(
        on_device, mesh=mesh, in_specs=in_specs, out_specs=out_specs, check_vma=False
    )
```

profile of v0, /device:TPU:8, one launch (start us, length us, event | category | flops | bytes accessed | tf_op | source)
XLA Modules:
  0.0 334.4 jit_solution(4841747790055246149)
XLA Ops:
  6.5 0.0 all-gather.2.cloned.1.call-start
  6.5 0.9 fusion.10
  7.5 1.5 fusion.11
  9.0 0.0 copy-start.1
  9.0 0.0 all-gather.2.cloned.1.call-update
  9.0 0.0 reduce-scatter.2.cloned.1.call-start
  9.0 7.7 %collective-permute-start.3 = (bf16[24,1024]{1,0:T(8,128)(2,1)}, bf16[24,1024]{1,0:T(8,128)(2,1)S(1)}, u32[]{:S(2)}, u32[]{:S(2)}) collective-permute-start(bf16[24,1024]{1,0:T(8,128)(2,1)} %fusion.11), channel_id=1, source_target_pairs={{64,0},{96,32},{128,64},{160,96},{192,128},{224,160},{256,192},{28... | collective-permute-start | bytes 147464 | tf_op jit(solution)/shard_map/ppermute | solution.py:15
  16.8 1.9 collective-permute-start.2
  18.7 2.4 collective-permute-start.1
  21.1 1.9 collective-permute-start
  23.1 1.5 fusion.25
  27.7 0.8 broadcast_compare_fusion
  28.4 0.1 broadcast_in_dim.50
  28.5 0.1 eq.80
  28.6 0.1 broadcast_in_dim.56
  28.7 0.1 eq.89
  28.8 0.1 broadcast_in_dim.54
  28.9 0.1 eq.86
  29.0 0.1 broadcast_in_dim.52
  29.0 0.1 eq.83
  29.2 0.1 broadcast_in_dim.48
  29.2 0.1 eq.77
  29.3 69.2 %all-gather.2.cloned.1.call-done = bf16[768,1024]{1,0:T(8,128)(2,1)} async-done(((bf16[24,1024]{1,0:T(8,128)(2,1)}), bf16[768,1024]{1,0:T(8,128)(2,1)}) %all-gather.2.cloned.1.call-update) | async-done | bytes 1572880 | tf_op jit(solution)/shard_map/all_gather | solution.py:44
  98.6 2.0 fusion.29
  100.5 0.0 copy-done.1
  100.6 0.0 copy-start
  100.6 0.6 fusion.23
  101.2 0.0 collective-permute-done
  101.2 0.8 copy-done
  102.0 0.5 fusion.30
  102.5 0.6 fusion.21
  103.1 0.0 collective-permute-done.1
  103.1 0.5 fusion.28
  103.7 0.6 fusion.19
  104.3 0.0 collective-permute-done.2
  104.3 0.5 fusion.27
  104.8 0.6 fusion.17
  105.4 0.0 collective-permute-done.3
  105.4 0.5 fusion.26
  106.0 1.9 add_convert_fusion
  107.9 0.0 reduce-scatter.2.cloned.1.call-update
  107.9 1.3 dynamic-slice
  109.9 72.2 %all-reduce = bf16[768]{0:T(1024)(128)(2,1)S(1)} all-reduce(bf16[768]{0:T(1024)(128)(2,1)S(1)} %add_convert_fusion.1), channel_id=3, replica_groups=mesh['wide'=16,'narrow'=32] {'narrow'}, use_global_device_ids=true, to_apply=%region_7.8.clone | all-reduce | flops 768 | bytes 3072
  182.1 0.1 dynamic-slice_convert_fusion
  182.1 143.9 %reduce-scatter.2.cloned.1.call-done = bf16[24,1024]{1,0:T(8,128)(2,1)} async-done(((bf16[768,1024]{1,0:T(8,128)(2,1)}), bf16[24,1024]{1,0:T(8,128)(2,1)}) %reduce-scatter.2.cloned.1.call-update) | async-done | bytes 49168 | tf_op jit(solution)/shard_map/reduce_scatter | solution.py:71
  326.0 1.5 convert_divide_fusion
  (4 shorter events, 0.0 us)
Async XLA Ops:
  6.5 92.0 %all-gather.2.cloned.1.call-start = ((), (), s32[]{:S(2)}) async-start(), calls=%async_computation.1 | async-start | bytes 1622016 | tf_op jit(solution)/shard_map/all_gather | solution.py:44
  9.0 91.6 %copy-start.1 = (bf16[24,1024]{1,0:T(8,128)(2,1)S(1)}, bf16[24,1024]{1,0:T(8,128)(2,1)}, u32[]{:S(2)}) copy-start(bf16[24,1024]{1,0:T(8,128)(2,1)} %fusion.11) | copy-start | bytes 147460
  9.0 317.1 %reduce-scatter.2.cloned.1.call-start = ((), (), s32[]{:S(2)}) async-start(), calls=%async_computation.2 | async-start | bytes 1622016 | tf_op jit(solution)/shard_map/reduce_scatter | solution.py:71
  9.0 96.4 %collective-permute-start.3 = (bf16[24,1024]{1,0:T(8,128)(2,1)}, bf16[24,1024]{1,0:T(8,128)(2,1)S(1)}, u32[]{:S(2)}, u32[]{:S(2)}) collective-permute-start(bf16[24,1024]{1,0:T(8,128)(2,1)} %fusion.11), channel_id=1, source_target_pairs={{64,0},{96,32},{128,64},{160,96},{192,128},{224,160},{256,192},{28... | collective-permute-start | bytes 147464 | tf_op jit(solution)/shard_map/ppermute | solution.py:15
  16.8 87.5 %collective-permute-start.2 = (bf16[24,1024]{1,0:T(8,128)(2,1)}, bf16[24,1024]{1,0:T(8,128)(2,1)S(1)}, u32[]{:S(2)}, u32[]{:S(2)}) collective-permute-start(bf16[24,1024]{1,0:T(8,128)(2,1)} %fusion.11), channel_id=1, source_target_pairs={{32,0},{64,32},{96,64},{128,96},{160,128},{192,160},{224,192},{256... | collective-permute-start | bytes 147464 | tf_op jit(solution)/shard_map/ppermute | solution.py:15
  18.7 84.4 %collective-permute-start.1 = (bf16[24,1024]{1,0:T(8,128)(2,1)}, bf16[24,1024]{1,0:T(8,128)(2,1)S(1)}, u32[]{:S(2)}, u32[]{:S(2)}) collective-permute-start(bf16[24,1024]{1,0:T(8,128)(2,1)} %fusion.11), channel_id=1, source_target_pairs={{0,32},{32,64},{64,96},{96,128},{128,160},{160,192},{192,224},{224... | collective-permute-start | bytes 147464 | tf_op jit(solution)/shard_map/ppermute | solution.py:15
  21.1 80.0 %collective-permute-start = (bf16[24,1024]{1,0:T(8,128)(2,1)}, bf16[24,1024]{1,0:T(8,128)(2,1)S(1)}, u32[]{:S(2)}, u32[]{:S(2)}) collective-permute-start(bf16[24,1024]{1,0:T(8,128)(2,1)} %fusion.11), channel_id=1, source_target_pairs={{0,64},{32,96},{64,128},{96,160},{128,192},{160,224},{192,256},{22... | collective-permute-start | bytes 147464 | tf_op jit(solution)/shard_map/ppermute | solution.py:15
  100.6 1.4 copy-start
Sparse Core Ops, SparseCore 0:
  10.5 88.0 all-gather.1
  108.1 217.9 reduce-scatter.1
where the time goes:
time: 335 us; the launch traced here: 334 us
  waiting for transfers between devices  213 us (64%)
  blocking collectives  72.2 us (22%)
  between operations  17.3 us (5%)
  starting transfers between devices  14 us (4%)
  matrix products  8.42 us (3%)
  other arithmetic  4.81 us (1%)
  local copies, waits for them, and re-layouts  4.48 us (1%)
    reduce_scatter x1, waiting for transfers between devices, on_device(): lax.psum_scatter(numerator.astype(jnp.bfloat16), 'narrow', scatter_dimens...  144 us
    unnamed x1, blocking collectives  72.2 us
    all_gather x1, waiting for transfers between devices, on_device(): group = lax.all_gather(normed, 'narrow', axis=0, tiled=True)  69.2 us
    ppermute x4, starting transfers between devices, from_behind(): return lax.ppermute(block, axis, route)  14 us
  transfers between devices with their start and end apart: 6, of which 2 were waited for; matrix products, arithmetic and copies ran while one was open for 3% of the time, Pallas kernels for 0%

commit v1 on v0

--- a/solution.py
+++ b/solution.py
@@ -41,7 +41,9 @@
     wide_at = lax.axis_index("wide")
     narrow_at = lax.axis_index("narrow")
     normed = normalize(embeddings)
-    group = lax.all_gather(normed, "narrow", axis=0, tiled=True)
+    group = jnp.concatenate(
+        lax.all_to_all(jnp.stack([normed] * lax.axis_size("narrow")), "narrow", 0, 0), axis=0
+    )
     rows_all = group.shape[0]
     first_block = wide_at * n_narrow
     group_clusters = lax.dynamic_slice_in_dim(cluster, first_block, n_narrow)

time: 335 us -> 297 us (0.89)
  waiting for transfers between devices: 213 us -> 169 us
  starting transfers between devices: 14 us -> 23.5 us
    all_gather x1 -> x0, waiting for transfers between devices: 69.2 us -> none  [on_device(): group = lax.all_gather(normed, 'narrow', axis=0, tiled=True)]
    all_to_all x0 -> x1, waiting for transfers between devices: none -> 24 us  [on_device(): lax.all_to_all(jnp.stack([normed] * lax.axis_size('narrow')), 'narrow', 0...]
    all_to_all x0 -> x1, starting transfers between devices: none -> 13.3 us  [on_device(): lax.all_to_all(jnp.stack([normed] * lax.axis_size('narrow')), 'narrow', 0...]
    ppermute x4, starting transfers between devices: 14 us -> 10.2 us  [from_behind(): return lax.ppermute(block, axis, route)]
where the time goes in v1:
time: 297 us; the launch traced here: 296 us
  waiting for transfers between devices  169 us (57%)
  blocking collectives  71.1 us (24%)
  starting transfers between devices  23.5 us (8%)
  between operations  17.4 us (6%)
  matrix products  7.01 us (2%)
  local copies, waits for them, and re-layouts  4.18 us (1%)
  other arithmetic  3.51 us (1%)
    reduce_scatter x1, waiting for transfers between devices, on_device(): lax.psum_scatter(numerator.astype(jnp.bfloat16), 'narrow', scatter_dimens...  145 us
    unnamed x1, blocking collectives  71.1 us
    all_to_all x1, waiting for transfers between devices, on_device(): lax.all_to_all(jnp.stack([normed] * lax.axis_size('narrow')), 'narrow', 0...  24 us
    all_to_all x1, starting transfers between devices, on_device(): lax.all_to_all(jnp.stack([normed] * lax.axis_size('narrow')), 'narrow', 0...  13.3 us
    ppermute x4, starting transfers between devices, from_behind(): return lax.ppermute(block, axis, route)  10.2 us
  transfers between devices with their start and end apart: 6, of which 2 were waited for; matrix products, arithmetic and copies ran while one was open for 3% of the time, Pallas kernels for 0%

profile of v1, /device:TPU:8, one launch (start us, length us, event | category | flops | bytes accessed | tf_op | source)
XLA Modules:
  0.0 296.2 jit_solution(9174819178088892717)
XLA Ops:
  6.5 0.9 fusion.10
  7.5 0.9 fusion.11
  8.3 1.3 stack.2
  9.7 0.0 copy-start
  9.7 13.3 %all-to-all-start = ((bf16[32,24,1024]{2,1,0:T(8,128)(2,1)}), bf16[32,24,1024]{2,1,0:T(8,128)(2,1)S(1)}, u32[]{:S(2)}, u32[]{:S(2)}) async-start(bf16[32,24,1024]{2,1,0:T(8,128)(2,1)} %stack.2), calls=%async_computation | async-start | bytes 3145728 | tf_op jit(solution)/shard_map/all_to_all | solution.py:45
  23.0 0.0 reduce-scatter.2.cloned.1.call-start
  23.1 2.4 collective-permute-start.3
  25.4 1.9 collective-permute-start.2
  27.3 2.4 collective-permute-start.1
  29.8 3.5 %collective-permute-start = (bf16[24,1024]{1,0:T(8,128)(2,1)S(1)}, bf16[24,1024]{1,0:T(8,128)(2,1)S(1)}, u32[]{:S(2)}, u32[]{:S(2)}) collective-permute-start(bf16[24,1024]{1,0:T(8,128)(2,1)S(1)} %fusion.11), channel_id=1, source_target_pairs={{0,64},{32,96},{64,128},{96,160},{128,192},{160,224},{192,256},{22... | collective-permute-start | bytes 147464 | tf_op jit(solution)/shard_map/ppermute | solution.py:15
  33.3 0.0 copy-done
  33.3 0.7 fusion.25
  37.1 0.1 broadcast_compare_fusion
  37.2 0.1 broadcast_in_dim.50
  37.3 0.1 eq.80
  37.4 0.1 broadcast_in_dim.56
  37.5 0.1 eq.89
  37.6 0.1 broadcast_in_dim.54
  37.7 0.1 eq.86
  37.8 0.1 broadcast_in_dim.52
  37.8 0.1 eq.83
  37.9 0.1 broadcast_in_dim.48
  38.0 0.1 eq.77
  38.1 24.0 %all-to-all-done = bf16[32,24,1024]{2,1,0:T(8,128)(2,1)S(1)} async-done(((bf16[32,24,1024]{2,1,0:T(8,128)(2,1)}), bf16[32,24,1024]{2,1,0:T(8,128)(2,1)S(1)}, u32[]{:S(2)}, u32[]{:S(2)}) %all-to-all-start) | async-done | bytes 1572896 | tf_op jit(solution)/shard_map/all_to_all | solution.py:45
  62.1 0.5 fusion.29
  62.7 0.6 fusion.23
  63.2 0.0 collective-permute-done.1
  63.3 0.5 fusion.28
  63.8 0.6 fusion.19
  64.4 0.0 collective-permute-done
  64.4 0.5 fusion.30
  65.0 0.6 fusion.21
  65.6 0.0 collective-permute-done.2
  65.6 0.5 fusion.27
  66.1 0.6 fusion.17
  66.7 0.0 collective-permute-done.3
  66.7 0.5 fusion.26
  67.3 1.9 add_convert_fusion
  69.2 0.0 reduce-scatter.2.cloned.1.call-update
  69.2 1.3 dynamic-slice
  71.2 71.1 %all-reduce = bf16[768]{0:T(1024)(128)(2,1)S(1)} all-reduce(bf16[768]{0:T(1024)(128)(2,1)S(1)} %add_convert_fusion.1), channel_id=3, replica_groups=mesh['wide'=16,'narrow'=32] {'narrow'}, use_global_device_ids=true, to_apply=%region_7.8.clone | all-reduce | flops 768 | bytes 3072
  142.3 0.1 dynamic-slice_convert_fusion
  142.4 145.4 %reduce-scatter.2.cloned.1.call-done = bf16[24,1024]{1,0:T(8,128)(2,1)} async-done(((bf16[768,1024]{1,0:T(8,128)(2,1)}), bf16[24,1024]{1,0:T(8,128)(2,1)}) %reduce-scatter.2.cloned.1.call-update) | async-done | bytes 49168 | tf_op jit(solution)/shard_map/reduce_scatter | solution.py:73
  287.8 1.5 convert_divide_fusion
  (4 shorter events, 0.0 us)
Async XLA Ops:
  9.7 23.6 %copy-start = (s32[512]{0:T(512)S(1)}, s32[512]{0:T(512)}, u32[]{:S(2)}) copy-start(s32[512]{0:T(512)} %param.3) | copy-start | bytes 6148
  9.7 52.4 %all-to-all-start = ((bf16[32,24,1024]{2,1,0:T(8,128)(2,1)}), bf16[32,24,1024]{2,1,0:T(8,128)(2,1)S(1)}, u32[]{:S(2)}, u32[]{:S(2)}) async-start(bf16[32,24,1024]{2,1,0:T(8,128)(2,1)} %stack.2), calls=%async_computation | async-start | bytes 3145728 | tf_op jit(solution)/shard_map/all_to_all | solution.py:45
  23.0 264.8 %reduce-scatter.2.cloned.1.call-start = ((), (), s32[]{:S(2)}) async-start(), calls=%async_computation.2 | async-start | bytes 1622016 | tf_op jit(solution)/shard_map/reduce_scatter | solution.py:73
  23.1 43.7 %collective-permute-start.3 = (bf16[24,1024]{1,0:T(8,128)(2,1)S(1)}, bf16[24,1024]{1,0:T(8,128)(2,1)S(1)}, u32[]{:S(2)}, u32[]{:S(2)}) collective-permute-start(bf16[24,1024]{1,0:T(8,128)(2,1)S(1)} %fusion.11), channel_id=1, source_target_pairs={{64,0},{96,32},{128,64},{160,96},{192,128},{224,160},{256,192},{28... | collective-permute-start | bytes 147464 | tf_op jit(solution)/shard_map/ppermute | solution.py:15
  25.4 40.2 %collective-permute-start.2 = (bf16[24,1024]{1,0:T(8,128)(2,1)S(1)}, bf16[24,1024]{1,0:T(8,128)(2,1)S(1)}, u32[]{:S(2)}, u32[]{:S(2)}) collective-permute-start(bf16[24,1024]{1,0:T(8,128)(2,1)S(1)} %fusion.11), channel_id=1, source_target_pairs={{32,0},{64,32},{96,64},{128,96},{160,128},{192,160},{224,192},{256... | collective-permute-start | bytes 147464 | tf_op jit(solution)/shard_map/ppermute | solution.py:15
  27.3 35.9 %collective-permute-start.1 = (bf16[24,1024]{1,0:T(8,128)(2,1)S(1)}, bf16[24,1024]{1,0:T(8,128)(2,1)S(1)}, u32[]{:S(2)}, u32[]{:S(2)}) collective-permute-start(bf16[24,1024]{1,0:T(8,128)(2,1)S(1)} %fusion.11), channel_id=1, source_target_pairs={{0,32},{32,64},{64,96},{96,128},{128,160},{160,192},{192,224},{224... | collective-permute-start | bytes 147464 | tf_op jit(solution)/shard_map/ppermute | solution.py:15
  29.8 34.7 %collective-permute-start = (bf16[24,1024]{1,0:T(8,128)(2,1)S(1)}, bf16[24,1024]{1,0:T(8,128)(2,1)S(1)}, u32[]{:S(2)}, u32[]{:S(2)}) collective-permute-start(bf16[24,1024]{1,0:T(8,128)(2,1)S(1)} %fusion.11), channel_id=1, source_target_pairs={{0,64},{32,96},{64,128},{96,160},{128,192},{160,224},{192,256},{22... | collective-permute-start | bytes 147464 | tf_op jit(solution)/shard_map/ppermute | solution.py:15
Sparse Core Ops, SparseCore 0:
  69.3 218.4 reduce-scatter.1
